TPU v7x, 256 devices: a whole 4x4x8 slice. The times are simulated.
256 devices in a mesh: cube: 64 (over y, z_lo, x, core), panel: 4 (over z_hi).
Axes of the slice: x: 4, y: 4, z: 8 (z_hi: 4, z_lo: 2; z = z_hi * 2 + z_lo), core: 2. Of those that a mesh axis runs over, the one named last changes fastest.
Arguments:
- leaf_updates: float32 [32768, 4096], P(('cube', 'panel')), as said below
- extend_maps: int32 [14, 4096], replicated, may hold values from 0 to 4607, as said below
- front_diagonal: float32 [7, 4608], replicated, may hold values from 0.5 to 2
- pivot_order: int32 [512], replicated, may hold values from 0 to 511, each once
- coupling_rows: bfloat16 [65536, 4608], P(('cube', 'panel')), may hold values from -0.1796875 to 0.1796875
- coupling_owner: int32 [65536, 1], P(('cube', 'panel')), may hold values from 0 to 255; in each aligned block of 256 rows (0 to 255, 256 to 511, ...) at most 2 rows name the same one
- coupling_slot: int32 [65536], P(('cube', 'panel')), may hold values from 0 to 15
Outputs:
- root_factor: bfloat16 [4096, 512], P(('cube', 'panel'))
- root_update: float32 [4096, 4096], P(('cube', 'panel'))
Inputs may be any that keep to these rules, and one draw needn't show every extreme that they name: leaf_updates: each of the 8 blocks of 4096 rows is symmetric positive definite. `extend_maps`: each row names distinct indices. For a child h of its parent (h = row parity) at merge level j, with g = 8 * 2 ** j, r = 4096 // (2 * g * 4) and k = 512 // (2 * g * 4): its indices fall in aligned blocks of 2 * r, block number s * 4 + p; the first r of a block name front indices of parent block (h * g + s) * 4 + p, the other r those of parent block ((1 - h) * g + s) * 4 + p, where parent block u holds pivots u * k to u * k + k - 1 and indices 512 + u * r to 512 + u * r + r - 1. `coupling_owner`: within the rows of one device, no owner is named by more than 2 rows.
All inputs are finite; a program needn't handle non-finite values.
Results may differ from a plain program's by a relative error of at most 0.0065.
Values may be sent and summed in bfloat16 or wider, within the bound.
A program may use at most 128 MiB of HBM per device.

v0:
```python
import jax
import jax.numpy as jnp
from jax import lax
from jax.sharding import PartitionSpec as P

CAP = 2


def from_partner(shard, axis, stride):
    return lax.ppermute(shard, axis, [(i, i ^ 1 << stride) for i in range(lax.axis_size(axis))])


def route_rows(coupling_rows, coupling_owner, coupling_slot, cubes, panels, root_rows):
    owners = coupling_owner[:, 0]
    owner_count = cubes * panels
    owner_hits = (owners[:, None] == jnp.arange(owner_count, dtype=jnp.int32)[None, :]).astype(
        jnp.int32
    )
    earlier = jnp.sum((jnp.cumsum(owner_hits, axis=0) - owner_hits) * owner_hits, axis=1)
    target = owners * CAP + earlier
    row_width = coupling_rows.shape[1]
    outgoing = jnp.zeros((owner_count * CAP, row_width), jnp.bfloat16).at[target].set(coupling_rows)
    slot_marks = (coupling_slot[:, None] == jnp.arange(root_rows, dtype=jnp.int32)[None, :]).astype(
        jnp.bfloat16
    )
    labels = jnp.zeros((owner_count * CAP, root_rows), jnp.bfloat16).at[target].set(slot_marks)
    outgoing = outgoing.reshape(cubes, panels, CAP, row_width)
    labels = labels.reshape(cubes, panels, CAP, root_rows)
    got_rows, got_labels = (
        lax.all_to_all(
            lax.all_to_all(outgoing, "cube", split_axis=0, concat_axis=0, tiled=True),
            "panel",
            split_axis=1,
            concat_axis=1,
            tiled=True,
        ),
        lax.all_to_all(
            lax.all_to_all(labels, "cube", split_axis=0, concat_axis=0, tiled=True),
            "panel",
            split_axis=1,
            concat_axis=1,
            tiled=True,
        ),
    )
    return jnp.einsum("abcr,abcf->rf", got_labels, got_rows, preferred_element_type=jnp.float32)


def place_rows(
    child_rows, child_map, block_start, parent_block, piv_rows, upd_rows, pivots, order_full
):
    targets = lax.dynamic_slice_in_dim(child_map, block_start, upd_rows)
    slots = jnp.where(
        targets < pivots,
        targets - parent_block * piv_rows,
        piv_rows + targets - pivots - parent_block * upd_rows,
    )
    source = (
        jnp.full((piv_rows + upd_rows,), -1, jnp.int32)
        .at[slots]
        .set(jnp.arange(upd_rows, dtype=jnp.int32))
    )
    columns = (
        jnp.full((order_full,), -1, jnp.int32)
        .at[child_map]
        .set(jnp.arange(child_map.shape[0], dtype=jnp.int32))
    )
    picked = jnp.take(child_rows, jnp.maximum(source, 0), axis=0)
    picked = jnp.take(picked, jnp.maximum(columns, 0), axis=1)
    present = (source >= 0)[:, None] & (columns >= 0)[None, :]
    return jnp.where(present, picked, 0.0)


def pair_join(mine, partner, cube_at, bit_step):
    upper_half = cube_at // 2**bit_step % 2
    return jnp.where(
        upper_half == 0, jnp.concatenate([mine, partner], 0), jnp.concatenate([partner, mine], 0)
    )


def body(
    leaf_updates,
    extend_maps,
    front_diagonal,
    pivot_order,
    coupling_rows,
    coupling_owner,
    coupling_slot,
):
    cubes = lax.axis_size("cube")
    panels = lax.axis_size("panel")
    cube_bits = cubes.bit_length() - 1
    cube_at = lax.axis_index("cube")
    panel_at = lax.axis_index("panel")
    row_width = leaf_updates.shape[1]
    pivots = pivot_order.shape[0]
    order_full = front_diagonal.shape[1]
    assembly = route_rows(
        coupling_rows, coupling_owner, coupling_slot, cubes, panels, row_width // (cubes * panels)
    )
    columns_all = jnp.arange(order_full, dtype=jnp.int32)
    children = leaf_updates
    map_base = 0
    diag_base = 0
    factor = None
    for merge_level in range(3):
        level_bit = cube_bits - 3 + merge_level
        group_size = 2 ** (level_bit + 1)
        half_group = group_size // 2
        position = cube_at % group_size
        front_at = cube_at // group_size
        child_side = position // half_group
        lower_pos = position % half_group
        upd_rows = row_width // (group_size * panels)
        piv_rows = pivots // (group_size * panels)
        child_block = lower_pos * panels + panel_at
        parent_block = position * panels + panel_at
        incoming = from_partner(children[upd_rows:], "cube", level_bit)
        own_map = jnp.take(extend_maps, map_base + 2 * front_at + child_side, axis=0)
        other_map = jnp.take(extend_maps, map_base + 2 * front_at + 1 - child_side, axis=0)
        block_start = child_block * 2 * upd_rows
        front_rows = place_rows(
            children[:upd_rows],
            own_map,
            block_start,
            parent_block,
            piv_rows,
            upd_rows,
            pivots,
            order_full,
        )
        front_rows = front_rows + place_rows(
            incoming,
            other_map,
            block_start + upd_rows,
            parent_block,
            piv_rows,
            upd_rows,
            pivots,
            order_full,
        )
        slot_ids = jnp.arange(piv_rows + upd_rows, dtype=jnp.int32)
        global_rows = jnp.where(
            slot_ids < piv_rows,
            parent_block * piv_rows + slot_ids,
            pivots + parent_block * upd_rows + slot_ids - piv_rows,
        )
        diag_row = jnp.take(front_diagonal, diag_base + front_at, axis=0)
        front_rows = front_rows + jnp.where(
            columns_all[None, :] == global_rows[:, None],
            jnp.take(diag_row, global_rows)[:, None],
            0.0,
        )
        pivot_rows = front_rows[:piv_rows, :pivots]
        update_rows = front_rows[piv_rows:]
        if merge_level == 2:
            update_rows = update_rows + assembly
        pivot_block = lax.all_gather(pivot_rows, "panel", axis=0, tiled=True)
        for bit_step in range(level_bit + 1):
            partner = from_partner(pivot_block, "cube", bit_step)
            pivot_block = pair_join(pivot_block, partner, cube_at, bit_step)
        coupled = update_rows[:, :pivots]
        if merge_level == 2:
            pivot_block = jnp.take(jnp.take(pivot_block, pivot_order, axis=0), pivot_order, axis=1)
            coupled = jnp.take(coupled, pivot_order, axis=1)
        chol_lower = jnp.linalg.cholesky(pivot_block)
        factor = lax.linalg.triangular_solve(
            chol_lower, coupled, left_side=False, lower=True, transpose_a=True
        ).astype(jnp.bfloat16)
        contract = (((1,), (1,)), ((), ()))
        collected = lax.all_gather(factor, "panel", axis=0, tiled=True)
        for bit_step in range(level_bit + 1):
            partner = from_partner(collected, "cube", bit_step)
            collected = pair_join(collected, partner, cube_at, bit_step)
        product = lax.dot_general(factor, collected, contract, preferred_element_type=jnp.float32)
        children = update_rows[:, pivots:] - product
        map_base += 8 // 2**merge_level
        diag_base += 4 // 2**merge_level
    return (factor, children)


def solution(mesh):
    return jax.shard_map(
        body,
        mesh=mesh,
        in_specs=(
            P(("cube", "panel"), None),
            P(),
            P(),
            P(),
            P(("cube", "panel"), None),
            P(("cube", "panel"), None),
            P(("cube", "panel")),
        ),
        out_specs=(P(("cube", "panel"), None), P(("cube", "panel"), None)),
        check_vma=False,
    )
```

profile of v0, /device:TPU:2, one launch (start us, length us, event | category | flops | bytes accessed | tf_op | source)
XLA Modules:
  0.0 1203.2 jit_solution(4935917101445240276)
XLA Ops:
  7.6 15.5 %scatter_custom_fusion.5 = s32[4608]{0:T(1024)S(1)} fusion(s32[4096]{0:T(1024)S(1)} %compare_select_fusion.3, s32[4096]{0:T(1024)S(1)} %iota.179, s32[]{:T(128)} %constant.591.clone.1), kind=kCustom, calls=%fused_computation.332 | custom fusion | bytes 18436 | tf_op jit(solution)/shard_map/scatter | solution.py:65
  40.1 15.5 %scatter_custom_fusion.7 = s32[4608]{0:T(1024)S(1)} fusion(s32[4096]{0:T(1024)S(1)} %compare_select_fusion.2, s32[4096]{0:T(1024)S(1)} %iota.181, s32[]{:T(128)} %constant.591.clone.1), kind=kCustom, calls=%fused_computation.330 | custom fusion | bytes 18436 | tf_op jit(solution)/shard_map/scatter | solution.py:65
  79.5 16.4 %all_gather.18 = f32[32,512]{1,0:T(8,128)S(1)} all-gather(f32[8,512]{1,0:T(8,128)S(1)} %slice.288), channel_id=1, replica_groups=mesh['cube'=64,'panel'=4] {'panel'}, dimensions={0}, use_global_device_ids=true | all-gather | bytes 81920 | tf_op jit(solution)/shard_map/all_gather | solution.py:157
  154.1 11.7 cholesky.393
  178.7 11.7 cholesky.414
  226.6 39.3 %custom-call.29 = f32[4,128,128]{1,2,0:T(8,128)S(1)} custom-call(f32[4,128,128]{2,1,0:T(8,128)S(1)} %get-tuple-element.34), custom_call_target="InvertDiagBlocksLowerTriangular" | custom-call | tf_op jit(solution)/shard_map/triangular_solve | solution.py:166
  270.6 14.9 %all_gather.19 = bf16[256,512]{1,0:T(8,128)(2,1)S(1)} all-gather(bf16[64,512]{1,0:T(8,128)(2,1)S(1)} %pad_maximum_fusion), channel_id=1, replica_groups=mesh['cube'=64,'panel'=4] {'panel'}, dimensions={0}, use_global_device_ids=true | all-gather | bytes 327680 | tf_op jit(solution)/shard_map/all_gather | solution.py:170
  287.9 13.4 %collective-permute-done.6 = bf16[512,512]{1,0:T(8,128)(2,1)S(1)} collective-permute-done((bf16[512,512]{1,0:T(8,128)(2,1)S(1)}, bf16[512,512]{1,0:T(8,128)(2,1)S(1)}, u32[]{:S(2)}, u32[]{:S(2)}) %collective-permute-start.6) | collective-permute-done | bytes 524320 | tf_op jit(solution)/shard_map/ppermute | solution.py:10
  304.8 15.5 %scatter_custom_fusion.3 = s32[4608]{0:T(1024)S(1)} fusion(s32[4096]{0:T(1024)S(1)} %compare_select_fusion.4, s32[4096]{0:T(1024)S(1)} %iota.177, s32[]{:T(128)} %constant.591.clone.1), kind=kCustom, calls=%fused_computation.334 | custom fusion | bytes 18436 | tf_op jit(solution)/shard_map/scatter | solution.py:65
  321.0 15.5 %scatter_custom_fusion.9 = s32[4608]{0:T(1024)S(1)} fusion(s32[4096]{0:T(1024)S(1)} %compare_select_fusion.1, s32[4096]{0:T(1024)S(1)} %iota.189, s32[]{:T(128)} %constant.591.clone.1), kind=kCustom, calls=%fused_computation.328 | custom fusion | bytes 18436 | tf_op jit(solution)/shard_map/scatter | solution.py:65
  340.5 45.0 %collective-permute-done.8 = bf16[2048,512]{1,0:T(8,128)(2,1)} collective-permute-done((bf16[2048,512]{1,0:T(8,128)(2,1)}, bf16[2048,512]{1,0:T(8,128)(2,1)}, u32[]{:S(2)}, u32[]{:S(2)}) %collective-permute-start.8) | collective-permute-done | bytes 2097184 | tf_op jit(solution)/shard_map/ppermute | solution.py:10
  421.3 13.7 %all-gather = f32[4,4,512]{2,1,0:T(4,128)S(1)} all-gather(f32[1,4,512]{2,1,0:T(4,128)S(1)} %slice_bitcast_fusion.24), channel_id=1, replica_groups=mesh['cube'=64,'panel'=4] {'panel'}, dimensions={0}, use_global_device_ids=true | all-gather | bytes 40960 | tf_op jit(solution)/shard_map/all_gather | solution.py:157
  594.2 39.3 %custom-call.30 = f32[4,128,128]{1,2,0:T(8,128)S(1)} custom-call(f32[4,128,128]{2,1,0:T(8,128)S(1)} %get-tuple-element.42), custom_call_target="InvertDiagBlocksLowerTriangular" | custom-call | tf_op jit(solution)/shard_map/triangular_solve | solution.py:166
  635.1 13.8 %all_gather.21 = bf16[128,512]{1,0:T(8,128)(2,1)S(1)} all-gather(bf16[32,512]{1,0:T(8,128)(2,1)S(1)} %pad_maximum_fusion.3), channel_id=1, replica_groups=mesh['cube'=64,'panel'=4] {'panel'}, dimensions={0}, use_global_device_ids=true | all-gather | bytes 163840 | tf_op jit(solution)/shard_map/all_gather | solution.py:170
  661.5 12.6 %collective-permute-done.17 = bf16[512,512]{1,0:T(8,128)(2,1)S(1)} collective-permute-done((bf16[512,512]{1,0:T(8,128)(2,1)S(1)}, bf16[512,512]{1,0:T(8,128)(2,1)S(1)}, u32[]{:S(2)}, u32[]{:S(2)}) %collective-permute-start.17) | collective-permute-done | bytes 524320 | tf_op jit(solution)/shard_map/ppermute | solution.py:10
  677.0 15.5 %scatter_custom_fusion.1 = s32[4608]{0:T(1024)S(1)} fusion(s32[4096]{0:T(1024)S(1)} %compare_select_fusion.5, s32[4096]{0:T(1024)S(1)} %iota.175, s32[]{:T(128)} %constant.591.clone.1), kind=kCustom, calls=%fused_computation.336 | custom fusion | bytes 18436 | tf_op jit(solution)/shard_map/scatter | solution.py:65
  693.2 15.5 %scatter_custom_fusion.11 = s32[4608]{0:T(1024)S(1)} fusion(s32[4096]{0:T(1024)S(1)} %compare_select_fusion, s32[4096]{0:T(1024)S(1)} %iota.197, s32[]{:T(128)} %constant.591.clone.1), kind=kCustom, calls=%fused_computation.326 | custom fusion | bytes 18436 | tf_op jit(solution)/shard_map/scatter | solution.py:65
  723.7 32.9 %collective-permute-done.19 = bf16[2048,512]{1,0:T(8,128)(2,1)} collective-permute-done((bf16[2048,512]{1,0:T(8,128)(2,1)}, bf16[2048,512]{1,0:T(8,128)(2,1)}, u32[]{:S(2)}, u32[]{:S(2)}) %collective-permute-start.19) | collective-permute-done | bytes 2097184 | tf_op jit(solution)/shard_map/ppermute | solution.py:10
  796.0 110.7 %all-gather.1 = f32[4,2,512]{2,1,0:T(2,128)S(1)} all-gather(f32[1,2,512]{2,1,0:T(2,128)S(1)} %slice_bitcast_fusion.25), channel_id=1, replica_groups=mesh['cube'=64,'panel'=4] {'panel'}, dimensions={0}, use_global_device_ids=true | all-gather | bytes 20480 | tf_op jit(solution)/shard_map/all_gather | solution.py:157
  1043.7 39.3 %custom-call.31 = f32[4,128,128]{1,2,0:T(8,128)S(1)} custom-call(f32[4,128,128]{2,1,0:T(8,128)S(1)} %get-tuple-element.50), custom_call_target="InvertDiagBlocksLowerTriangular" | custom-call | tf_op jit(solution)/shard_map/triangular_solve | solution.py:166
  1088.9 13.7 %all_gather.23 = bf16[64,512]{1,0:T(8,128)(2,1)S(1)} all-gather(bf16[16,512]{1,0:T(8,128)(2,1)S(1)} %pad_maximum_fusion.4), channel_id=1, replica_groups=mesh['cube'=64,'panel'=4] {'panel'}, dimensions={0}, use_global_device_ids=true | all-gather | bytes 81920 | tf_op jit(solution)/shard_map/all_gather | solution.py:170
  1119.0 12.2 %collective-permute-done.30 = bf16[512,512]{1,0:T(8,128)(2,1)S(1)} collective-permute-done((bf16[512,512]{1,0:T(8,128)(2,1)S(1)}, bf16[512,512]{1,0:T(8,128)(2,1)S(1)}, u32[]{:S(2)}, u32[]{:S(2)}) %collective-permute-start.30) | collective-permute-done | bytes 524320 | tf_op jit(solution)/shard_map/ppermute | solution.py:10
  1132.0 22.4 %collective-permute-done.31 = bf16[1024,512]{1,0:T(8,128)(2,1)S(1)} collective-permute-done((bf16[1024,512]{1,0:T(8,128)(2,1)S(1)}, bf16[1024,512]{1,0:T(8,128)(2,1)S(1)}, u32[]{:S(2)}, u32[]{:S(2)}) %collective-permute-start.31) | collective-permute-done | bytes 1048608 | tf_op jit(solution)/shard_map/ppermute | solution.py:10
  1156.0 44.7 %collective-permute-done.32 = bf16[2048,512]{1,0:T(8,128)(2,1)S(1)} collective-permute-done((bf16[2048,512]{1,0:T(8,128)(2,1)S(1)}, bf16[2048,512]{1,0:T(8,128)(2,1)S(1)}, u32[]{:S(2)}, u32[]{:S(2)}) %collective-permute-start.32) | collective-permute-done | bytes 2097184 | tf_op jit(solution)/shard_map/ppermute | solution.py:10
  (423 shorter events, 615.8 us)
Async XLA Ops:
  3.3 54.8 %collective-permute-start = (f32[64,4096]{1,0:T(8,128)}, f32[64,4096]{1,0:T(8,128)S(1)}, u32[]{:S(2)}, u32[]{:S(2)}) collective-permute-start(f32[64,4096]{1,0:T(8,128)} %get-tuple-element.97), channel_id=1, source_target_pairs={{0,32},{4,36},{8,40},{12,44},{16,48},{20,52},{24,56},{28,60},{32,0... | collective-permute-start | bytes 3145736 | tf_op jit(solution)/shard_map/ppermute | solution.py:10
  106.5 9.1 collective-permute-start.3
  115.6 12.5 %collective-permute-start.4 = (f32[256,512]{0,1:T(8,128)S(1)}, f32[256,512]{0,1:T(8,128)S(1)}, u32[]{:S(2)}, u32[]{:S(2)}) collective-permute-start(f32[256,512]{0,1:T(8,128)S(1)} %maximum_select_fusion.15), channel_id=1, source_target_pairs={{0,32},{4,36},{8,40},{12,44},{16,48},{20,52},{24,56},{28,60},{32,0... | collective-permute-start | bytes 1572872 | tf_op jit(solution)/shard_map/ppermute | solution.py:10
  287.2 14.1 %collective-permute-start.6 = (bf16[512,512]{1,0:T(8,128)(2,1)S(1)}, bf16[512,512]{1,0:T(8,128)(2,1)S(1)}, u32[]{:S(2)}, u32[]{:S(2)}) collective-permute-start(bf16[512,512]{1,0:T(8,128)(2,1)S(1)} %maximum_select_fusion.16), channel_id=1, source_target_pairs={{0,8},{4,12},{8,0},{12,4},{16,24},{20,28},{24,16},{28,20},{32,40},... | collective-permute-start | bytes 1572872 | tf_op jit(solution)/shard_map/ppermute | solution.py:10
  301.8 34.8 %collective-permute-start.7 = (bf16[1024,512]{1,0:T(8,128)(2,1)S(1)}, bf16[1024,512]{1,0:T(8,128)(2,1)S(1)}, u32[]{:S(2)}, u32[]{:S(2)}) collective-permute-start(bf16[1024,512]{1,0:T(8,128)(2,1)S(1)} %maximum_select_fusion.10), channel_id=1, source_target_pairs={{0,16},{4,20},{8,24},{12,28},{16,0},{20,4},{24,8},{28,12},{32,48},... | collective-permute-start | bytes 3145736 | tf_op jit(solution)/shard_map/ppermute | solution.py:10
  338.6 46.9 %collective-permute-start.8 = (bf16[2048,512]{1,0:T(8,128)(2,1)}, bf16[2048,512]{1,0:T(8,128)(2,1)}, u32[]{:S(2)}, u32[]{:S(2)}) collective-permute-start(bf16[2048,512]{1,0:T(8,128)(2,1)} %maximum_select_fusion.6), channel_id=1, source_target_pairs={{0,32},{4,36},{8,40},{12,44},{16,48},{20,52},{24,56},{28,60},{32,0... | collective-permute-start | bytes 6291464 | tf_op jit(solution)/shard_map/ppermute | solution.py:10
  390.9 14.9 %collective-permute-start.9 = (f32[32,4096]{1,0:T(8,128)}, f32[32,4096]{1,0:T(8,128)S(1)}, u32[]{:S(2)}, u32[]{:S(2)}) collective-permute-start(f32[32,4096]{1,0:T(8,128)} %get-tuple-element.99), channel_id=1, source_target_pairs={{0,64},{4,68},{8,72},{12,76},{16,80},{20,84},{24,88},{28,92},{32,9... | collective-permute-start | bytes 1572872 | tf_op jit(solution)/shard_map/ppermute | solution.py:10
  436.7 8.5 collective-permute-start.11
  445.4 9.1 collective-permute-start.12
  461.4 26.3 %collective-permute-start.14 = (f32[256,512]{0,1:T(8,128)S(1)}, f32[256,512]{0,1:T(8,128)S(1)}, u32[]{:S(2)}, u32[]{:S(2)}) collective-permute-start(f32[256,512]{0,1:T(8,128)S(1)} %maximum_select_fusion.17), channel_id=1, source_target_pairs={{0,64},{4,68},{8,72},{12,76},{16,80},{20,84},{24,88},{28,92},{32,9... | collective-permute-start | bytes 1572872 | tf_op jit(solution)/shard_map/ppermute | solution.py:10
  464.1 84.5 %all-to-all-start = ((bf16[64,4,2,16]{3,2,1,0:T(2,128)(2,1)}), bf16[64,4,2,16]{3,2,1,0:T(2,128)(2,1)S(1)}, u32[]{:S(2)}, u32[]{:S(2)}) async-start(bf16[64,4,2,16]{3,2,1,0:T(2,128)(2,1)} %bitcast.45), calls=%async_computation | async-start | bytes 262144 | tf_op jit(solution)/shard_map/all_to_all | solution.py:38
  548.7 165.2 %all-to-all-start.2 = ((bf16[64,4,2,4608]{3,2,1,0:T(2,128)(2,1)}), bf16[64,4,2,4608]{3,2,1,0:T(2,128)(2,1)}, u32[]{:S(2)}, u32[]{:S(2)}) async-start(bf16[64,4,2,4608]{3,2,1,0:T(2,128)(2,1)} %reshape.273), calls=%async_computation.2 | async-start | bytes 9437184 | tf_op jit(solution)/shard_map/all_to_all | solution.py:31
  650.3 8.4 collective-permute-start.16
  658.9 15.1 %collective-permute-start.17 = (bf16[512,512]{1,0:T(8,128)(2,1)S(1)}, bf16[512,512]{1,0:T(8,128)(2,1)S(1)}, u32[]{:S(2)}, u32[]{:S(2)}) collective-permute-start(bf16[512,512]{1,0:T(8,128)(2,1)S(1)} %maximum_select_fusion.18), channel_id=1, source_target_pairs={{0,16},{4,20},{8,24},{12,28},{16,0},{20,4},{24,8},{28,12},{32,48},... | collective-permute-start | bytes 1572872 | tf_op jit(solution)/shard_map/ppermute | solution.py:10
  674.5 34.2 %collective-permute-start.18 = (bf16[1024,512]{1,0:T(8,128)(2,1)S(1)}, bf16[1024,512]{1,0:T(8,128)(2,1)S(1)}, u32[]{:S(2)}, u32[]{:S(2)}) collective-permute-start(bf16[1024,512]{1,0:T(8,128)(2,1)S(1)} %maximum_select_fusion.12), channel_id=1, source_target_pairs={{0,32},{4,36},{8,40},{12,44},{16,48},{20,52},{24,56},{28,60},{32,0... | collective-permute-start | bytes 3145736 | tf_op jit(solution)/shard_map/ppermute | solution.py:10
  710.7 46.0 %collective-permute-start.19 = (bf16[2048,512]{1,0:T(8,128)(2,1)}, bf16[2048,512]{1,0:T(8,128)(2,1)}, u32[]{:S(2)}, u32[]{:S(2)}) collective-permute-start(bf16[2048,512]{1,0:T(8,128)(2,1)} %maximum_select_fusion.7), channel_id=1, source_target_pairs={{0,64},{4,68},{8,72},{12,76},{16,80},{20,84},{24,88},{28,92},{32,9... | collective-permute-start | bytes 6291464 | tf_op jit(solution)/shard_map/ppermute | solution.py:10
  713.9 77.1 %all-to-all-start.1 = ((bf16[4,2,1024]{2,1,0:T(2,128)(2,1)}), bf16[4,2,1024]{2,1,0:T(2,128)(2,1)S(1)}, u32[]{:S(2)}, u32[]{:S(2)}) async-start(bf16[4,2,1024]{2,1,0:T(2,128)(2,1)} %reshape.834), calls=%async_computation.1 | async-start | bytes 32768 | tf_op jit(solution)/shard_map/all_to_all | solution.py:37
  761.3 16.2 %collective-permute-start.20 = (f32[16,4096]{1,0:T(8,128)S(1)}, f32[16,4096]{1,0:T(8,128)S(1)}, u32[]{:S(2)}, u32[]{:S(2)}) collective-permute-start(f32[16,4096]{1,0:T(8,128)S(1)} %get-tuple-element.101), channel_id=1, source_target_pairs={{0,128},{4,132},{8,136},{12,140},{16,144},{20,148},{24,152},{28,15... | collective-permute-start | bytes 786440 | tf_op jit(solution)/shard_map/ppermute | solution.py:10
  790.9 292.0 %all-to-all-start.3 = ((bf16[64,4,2,4608]{3,0,2,1:T(8,128)(2,1)}), bf16[64,4,2,4608]{3,0,2,1:T(8,128)(2,1)}, u32[]{:S(2)}, u32[]{:S(2)}) async-start(bf16[64,4,2,4608]{3,0,2,1:T(8,128)(2,1)} %copy.76), calls=%async_computation.3 | async-start | bytes 9437184 | tf_op jit(solution)/shard_map/all_to_all | solution.py:30
  931.3 10.8 collective-permute-start.26
  1109.6 9.1 collective-permute-start.29
  1118.9 12.3 %collective-permute-start.30 = (bf16[512,512]{1,0:T(8,128)(2,1)S(1)}, bf16[512,512]{1,0:T(8,128)(2,1)S(1)}, u32[]{:S(2)}, u32[]{:S(2)}) collective-permute-start(bf16[512,512]{1,0:T(8,128)(2,1)S(1)} %maximum_select_fusion.20), channel_id=1, source_target_pairs={{0,32},{4,36},{8,40},{12,44},{16,48},{20,52},{24,56},{28,60},{32,0... | collective-permute-start | bytes 1572872 | tf_op jit(solution)/shard_map/ppermute | solution.py:10
  1131.7 22.7 %collective-permute-start.31 = (bf16[1024,512]{1,0:T(8,128)(2,1)S(1)}, bf16[1024,512]{1,0:T(8,128)(2,1)S(1)}, u32[]{:S(2)}, u32[]{:S(2)}) collective-permute-start(bf16[1024,512]{1,0:T(8,128)(2,1)S(1)} %maximum_select_fusion.14), channel_id=1, source_target_pairs={{0,64},{4,68},{8,72},{12,76},{16,80},{20,84},{24,88},{28,92},{32,9... | collective-permute-start | bytes 3145736 | tf_op jit(solution)/shard_map/ppermute | solution.py:10
  1155.0 45.6 %collective-permute-start.32 = (bf16[2048,512]{1,0:T(8,128)(2,1)S(1)}, bf16[2048,512]{1,0:T(8,128)(2,1)S(1)}, u32[]{:S(2)}, u32[]{:S(2)}) collective-permute-start(bf16[2048,512]{1,0:T(8,128)(2,1)S(1)} %maximum_select_fusion.8), channel_id=1, source_target_pairs={{0,128},{4,132},{8,136},{12,140},{16,144},{20,148},{24,152},{28,15... | collective-permute-start | bytes 6291464 | tf_op jit(solution)/shard_map/ppermute | solution.py:10
  (26 other events, 541.8 us)
where the time goes:
time: 1210 us; the launch traced here: 1200 us
  other arithmetic  379 us (31%)
  waiting for transfers between devices  288 us (24%)
  local copies, waits for them, and re-layouts  245 us (20%)
  blocking collectives  183 us (15%)
  starting transfers between devices  59.1 us (5%)
  matrix products  38.3 us (3%)
    ppermute x33, waiting for transfers between devices, from_partner(): lax.ppermute(shard, axis, [(i, i ^ 1 << stride) for i in range(lax.axis_s...  288 us
    another operation x45, other arithmetic, body(): chol_lower = jnp.linalg.cholesky(pivot_block)  238 us
    all_gather x3, blocking collectives, body(): pivot_block = lax.all_gather(pivot_rows, 'panel', axis=0, tiled=True)  141 us
    another operation x10, other arithmetic, body(): lax.linalg.triangular_solve(chol_lower, coupled, left_side=False, lower=T...  119 us
    scatter x6, local copies, waits for them, and re-layouts, place_rows(): columns = jnp.full((order_full,), -1, jnp.int32).at[child_map].set(jnp.ar...  93.2 us
    gather x12, local copies, waits for them, and re-layouts, place_rows(): picked = jnp.take(picked, jnp.maximum(columns, 0), axis=1)  71 us
    all_gather x3, blocking collectives, body(): collected = lax.all_gather(factor, 'panel', axis=0, tiled=True)  42.4 us
    ppermute x33, starting transfers between devices, from_partner(): lax.ppermute(shard, axis, [(i, i ^ 1 << stride) for i in range(lax.axis_s...  33.2 us
  transfers between devices with their start and end apart: 37, of which 27 were waited for; matrix products, arithmetic and copies ran while one was open for 38% of the time, Pallas kernels for 0%

commit v1 on v0

--- a/solution.py
+++ b/solution.py
@@ -154,7 +154,9 @@
         update_rows = front_rows[piv_rows:]
         if merge_level == 2:
             update_rows = update_rows + assembly
-        pivot_block = lax.all_gather(pivot_rows, "panel", axis=0, tiled=True)
+        pivot_block = jnp.concatenate(
+            lax.all_to_all(jnp.stack([pivot_rows] * lax.axis_size("panel")), "panel", 0, 0), axis=0
+        )
         for bit_step in range(level_bit + 1):
             partner = from_partner(pivot_block, "cube", bit_step)
             pivot_block = pair_join(pivot_block, partner, cube_at, bit_step)

time: 1210 us -> 1260 us (1.041)
  waiting for transfers between devices: 288 us -> 383 us
  blocking collectives: 183 us -> 121 us
    all_gather x3 -> x0, blocking collectives: 141 us -> none  [body(): pivot_block = lax.all_gather(pivot_rows, 'panel', axis=0, tiled=True)]
    ppermute x33, waiting for transfers between devices: 288 us -> 381 us  [from_partner(): lax.ppermute(shard, axis, [(i, i ^ 1 << stride) for i in range(lax.axis_s...]
    all_gather x3, blocking collectives: 42.4 us -> 94.3 us  [body(): collected = lax.all_gather(factor, 'panel', axis=0, tiled=True)]
    all_to_all x0 -> x2, blocking collectives: none -> 26.9 us  [body(): lax.all_to_all(jnp.stack([pivot_rows] * lax.axis_size('panel')), 'panel',...]
  transfers between devices with their start and end apart: 37 -> 38, of which waited for: 27 -> 28; matrix products, arithmetic and copies ran while one was open for 38% -> 37% of each run, Pallas kernels for 0% -> 0%
where the time goes in v1:
time: 1260 us; the launch traced here: 1250 us
  waiting for transfers between devices  383 us (30%)
  other arithmetic  379 us (30%)
  local copies, waits for them, and re-layouts  246 us (20%)
  blocking collectives  121 us (10%)
  starting transfers between devices  68.2 us (5%)
  matrix products  38.1 us (3%)
    ppermute x33, waiting for transfers between devices, from_partner(): lax.ppermute(shard, axis, [(i, i ^ 1 << stride) for i in range(lax.axis_s...  381 us
    another operation x45, other arithmetic, body(): chol_lower = jnp.linalg.cholesky(pivot_block)  238 us
    another operation x10, other arithmetic, body(): lax.linalg.triangular_solve(chol_lower, coupled, left_side=False, lower=T...  119 us
    all_gather x3, blocking collectives, body(): collected = lax.all_gather(factor, 'panel', axis=0, tiled=True)  94.3 us
    scatter x6, local copies, waits for them, and re-layouts, place_rows(): columns = jnp.full((order_full,), -1, jnp.int32).at[child_map].set(jnp.ar...  93.2 us
    gather x12, local copies, waits for them, and re-layouts, place_rows(): picked = jnp.take(picked, jnp.maximum(columns, 0), axis=1)  71 us
    ppermute x33, starting transfers between devices, from_partner(): lax.ppermute(shard, axis, [(i, i ^ 1 << stride) for i in range(lax.axis_s...  38.7 us
    all_to_all x2, blocking collectives, body(): lax.all_to_all(jnp.stack([pivot_rows] * lax.axis_size('panel')), 'panel',...  26.9 us
  transfers between devices with their start and end apart: 38, of which 28 were waited for; matrix products, arithmetic and copies ran while one was open for 37% of the time, Pallas kernels for 0%

profile of v1, /device:TPU:2, one launch (start us, length us, event | category | flops | bytes accessed | tf_op | source)
XLA Modules:
  0.0 1246.1 jit_solution(10903557065661891784)
XLA Ops:
  7.6 15.5 %scatter_custom_fusion.5 = s32[4608]{0:T(1024)S(1)} fusion(s32[4096]{0:T(1024)S(1)} %compare_select_fusion.3, s32[4096]{0:T(1024)S(1)} %iota.179, s32[]{:T(128)} %constant.591.clone.1), kind=kCustom, calls=%fused_computation.332 | custom fusion | bytes 18436 | tf_op jit(solution)/shard_map/scatter | solution.py:65
  40.1 15.5 %scatter_custom_fusion.7 = s32[4608]{0:T(1024)S(1)} fusion(s32[4096]{0:T(1024)S(1)} %compare_select_fusion.2, s32[4096]{0:T(1024)S(1)} %iota.181, s32[]{:T(128)} %constant.591.clone.1), kind=kCustom, calls=%fused_computation.330 | custom fusion | bytes 18436 | tf_op jit(solution)/shard_map/scatter | solution.py:65
  79.5 15.6 %all_to_all.35 = f32[4,8,512]{2,1,0:T(8,128)S(1)} all-to-all(f32[4,8,512]{2,1,0:T(8,128)S(1)} %stack.6), channel_id=1, replica_groups=mesh['cube'=64,'panel'=4] {'panel'}, dimensions={0} | all-to-all | bytes 131072 | tf_op jit(solution)/shard_map/all_to_all | solution.py:158
  129.0 11.7 cholesky.374
  153.3 11.7 cholesky.393
  177.9 11.7 cholesky.414
  201.6 11.7 cholesky.431
  225.8 39.3 %custom-call.29 = f32[4,128,128]{1,2,0:T(8,128)S(1)} custom-call(f32[4,128,128]{2,1,0:T(8,128)S(1)} %get-tuple-element.34), custom_call_target="InvertDiagBlocksLowerTriangular" | custom-call | tf_op jit(solution)/shard_map/triangular_solve | solution.py:168
  269.8 14.1 %all_gather.9 = bf16[256,512]{1,0:T(8,128)(2,1)S(1)} all-gather(bf16[64,512]{1,0:T(8,128)(2,1)S(1)} %pad_maximum_fusion), channel_id=1, replica_groups=mesh['cube'=64,'panel'=4] {'panel'}, dimensions={0}, use_global_device_ids=true | all-gather | bytes 327680 | tf_op jit(solution)/shard_map/all_gather | solution.py:172
  286.2 13.4 %collective-permute-done.6 = bf16[512,512]{1,0:T(8,128)(2,1)S(1)} collective-permute-done((bf16[512,512]{1,0:T(8,128)(2,1)S(1)}, bf16[512,512]{1,0:T(8,128)(2,1)S(1)}, u32[]{:S(2)}, u32[]{:S(2)}) %collective-permute-start.6) | collective-permute-done | bytes 524320 | tf_op jit(solution)/shard_map/ppermute | solution.py:10
  303.1 15.5 %scatter_custom_fusion.3 = s32[4608]{0:T(1024)S(1)} fusion(s32[4096]{0:T(1024)S(1)} %compare_select_fusion.4, s32[4096]{0:T(1024)S(1)} %iota.177, s32[]{:T(128)} %constant.591.clone.1), kind=kCustom, calls=%fused_computation.334 | custom fusion | bytes 18436 | tf_op jit(solution)/shard_map/scatter | solution.py:65
  319.4 15.5 %scatter_custom_fusion.9 = s32[4608]{0:T(1024)S(1)} fusion(s32[4096]{0:T(1024)S(1)} %compare_select_fusion.1, s32[4096]{0:T(1024)S(1)} %iota.189, s32[]{:T(128)} %constant.591.clone.1), kind=kCustom, calls=%fused_computation.328 | custom fusion | bytes 18436 | tf_op jit(solution)/shard_map/scatter | solution.py:65
  338.9 44.9 %collective-permute-done.8 = bf16[2048,512]{1,0:T(8,128)(2,1)} collective-permute-done((bf16[2048,512]{1,0:T(8,128)(2,1)}, bf16[2048,512]{1,0:T(8,128)(2,1)}, u32[]{:S(2)}, u32[]{:S(2)}) %collective-permute-start.8) | collective-permute-done | bytes 2097184 | tf_op jit(solution)/shard_map/ppermute | solution.py:10
  585.6 39.3 %custom-call.30 = f32[4,128,128]{1,2,0:T(8,128)S(1)} custom-call(f32[4,128,128]{2,1,0:T(8,128)S(1)} %get-tuple-element.42), custom_call_target="InvertDiagBlocksLowerTriangular" | custom-call | tf_op jit(solution)/shard_map/triangular_solve | solution.py:168
  635.4 65.6 %all_gather.10 = bf16[128,512]{1,0:T(8,128)(2,1)S(1)} all-gather(bf16[32,512]{1,0:T(8,128)(2,1)S(1)} %pad_maximum_fusion.3), channel_id=1, replica_groups=mesh['cube'=64,'panel'=4] {'panel'}, dimensions={0}, use_global_device_ids=true | all-gather | bytes 163840 | tf_op jit(solution)/shard_map/all_gather | solution.py:172
  713.3 13.6 %collective-permute-done.17 = bf16[512,512]{1,0:T(8,128)(2,1)S(1)} collective-permute-done((bf16[512,512]{1,0:T(8,128)(2,1)S(1)}, bf16[512,512]{1,0:T(8,128)(2,1)S(1)}, u32[]{:S(2)}, u32[]{:S(2)}) %collective-permute-start.17) | collective-permute-done | bytes 524320 | tf_op jit(solution)/shard_map/ppermute | solution.py:10
  728.3 15.5 %scatter_custom_fusion.1 = s32[4608]{0:T(1024)S(1)} fusion(s32[4096]{0:T(1024)S(1)} %compare_select_fusion.5, s32[4096]{0:T(1024)S(1)} %iota.175, s32[]{:T(128)} %constant.591.clone.1), kind=kCustom, calls=%fused_computation.336 | custom fusion | bytes 18436 | tf_op jit(solution)/shard_map/scatter | solution.py:65
  744.5 15.5 %scatter_custom_fusion.11 = s32[4608]{0:T(1024)S(1)} fusion(s32[4096]{0:T(1024)S(1)} %compare_select_fusion, s32[4096]{0:T(1024)S(1)} %iota.197, s32[]{:T(128)} %constant.591.clone.1), kind=kCustom, calls=%fused_computation.326 | custom fusion | bytes 18436 | tf_op jit(solution)/shard_map/scatter | solution.py:65
  763.9 44.8 %collective-permute-done.19 = bf16[2048,512]{1,0:T(8,128)(2,1)} collective-permute-done((bf16[2048,512]{1,0:T(8,128)(2,1)}, bf16[2048,512]{1,0:T(8,128)(2,1)}, u32[]{:S(2)}, u32[]{:S(2)}) %collective-permute-start.19) | collective-permute-done | bytes 2097184 | tf_op jit(solution)/shard_map/ppermute | solution.py:10
  873.2 90.7 %collective-permute-done.24 = f32[64,512]{1,0:T(8,128)S(1)} collective-permute-done((f32[64,512]{1,0:T(8,128)S(1)}, f32[64,512]{1,0:T(8,128)S(1)}, u32[]{:S(2)}, u32[]{:S(2)}) %collective-permute-start.24) | collective-permute-done | bytes 131104 | tf_op jit(solution)/shard_map/ppermute | solution.py:10
  1085.6 39.3 %custom-call.31 = f32[4,128,128]{1,2,0:T(8,128)S(1)} custom-call(f32[4,128,128]{2,1,0:T(8,128)S(1)} %get-tuple-element.50), custom_call_target="InvertDiagBlocksLowerTriangular" | custom-call | tf_op jit(solution)/shard_map/triangular_solve | solution.py:168
  1130.9 14.6 %all_gather.11 = bf16[64,512]{1,0:T(8,128)(2,1)S(1)} all-gather(bf16[16,512]{1,0:T(8,128)(2,1)S(1)} %pad_maximum_fusion.4), channel_id=1, replica_groups=mesh['cube'=64,'panel'=4] {'panel'}, dimensions={0}, use_global_device_ids=true | all-gather | bytes 81920 | tf_op jit(solution)/shard_map/all_gather | solution.py:172
  1175.2 22.0 %collective-permute-done.31 = bf16[1024,512]{1,0:T(8,128)(2,1)S(1)} collective-permute-done((bf16[1024,512]{1,0:T(8,128)(2,1)S(1)}, bf16[1024,512]{1,0:T(8,128)(2,1)S(1)}, u32[]{:S(2)}, u32[]{:S(2)}) %collective-permute-start.31) | collective-permute-done | bytes 1048608 | tf_op jit(solution)/shard_map/ppermute | solution.py:10
  1199.4 44.2 %collective-permute-done.32 = bf16[2048,512]{1,0:T(8,128)(2,1)S(1)} collective-permute-done((bf16[2048,512]{1,0:T(8,128)(2,1)S(1)}, bf16[2048,512]{1,0:T(8,128)(2,1)S(1)}, u32[]{:S(2)}, u32[]{:S(2)}) %collective-permute-start.32) | collective-permute-done | bytes 2097184 | tf_op jit(solution)/shard_map/ppermute | solution.py:10
  (427 shorter events, 618.4 us)
Async XLA Ops:
  3.3 54.8 %collective-permute-start = (f32[64,4096]{1,0:T(8,128)}, f32[64,4096]{1,0:T(8,128)S(1)}, u32[]{:S(2)}, u32[]{:S(2)}) collective-permute-start(f32[64,4096]{1,0:T(8,128)} %get-tuple-element.97), channel_id=1, source_target_pairs={{0,32},{4,36},{8,40},{12,44},{16,48},{20,52},{24,56},{28,60},{32,0... | collective-permute-start | bytes 3145736 | tf_op jit(solution)/shard_map/ppermute | solution.py:10
  114.8 12.5 %collective-permute-start.4 = (f32[256,512]{0,1:T(8,128)S(1)}, f32[256,512]{0,1:T(8,128)S(1)}, u32[]{:S(2)}, u32[]{:S(2)}) collective-permute-start(f32[256,512]{0,1:T(8,128)S(1)} %maximum_select_fusion.15), channel_id=1, source_target_pairs={{0,32},{4,36},{8,40},{12,44},{16,48},{20,52},{24,56},{28,60},{32,0... | collective-permute-start | bytes 1572872 | tf_op jit(solution)/shard_map/ppermute | solution.py:10
  285.6 14.1 %collective-permute-start.6 = (bf16[512,512]{1,0:T(8,128)(2,1)S(1)}, bf16[512,512]{1,0:T(8,128)(2,1)S(1)}, u32[]{:S(2)}, u32[]{:S(2)}) collective-permute-start(bf16[512,512]{1,0:T(8,128)(2,1)S(1)} %maximum_select_fusion.16), channel_id=1, source_target_pairs={{0,8},{4,12},{8,0},{12,4},{16,24},{20,28},{24,16},{28,20},{32,40},... | collective-permute-start | bytes 1572872 | tf_op jit(solution)/shard_map/ppermute | solution.py:10
  300.1 34.8 %collective-permute-start.7 = (bf16[1024,512]{1,0:T(8,128)(2,1)S(1)}, bf16[1024,512]{1,0:T(8,128)(2,1)S(1)}, u32[]{:S(2)}, u32[]{:S(2)}) collective-permute-start(bf16[1024,512]{1,0:T(8,128)(2,1)S(1)} %maximum_select_fusion.10), channel_id=1, source_target_pairs={{0,16},{4,20},{8,24},{12,28},{16,0},{20,4},{24,8},{28,12},{32,48},... | collective-permute-start | bytes 3145736 | tf_op jit(solution)/shard_map/ppermute | solution.py:10
  336.9 46.9 %collective-permute-start.8 = (bf16[2048,512]{1,0:T(8,128)(2,1)}, bf16[2048,512]{1,0:T(8,128)(2,1)}, u32[]{:S(2)}, u32[]{:S(2)}) collective-permute-start(bf16[2048,512]{1,0:T(8,128)(2,1)} %maximum_select_fusion.6), channel_id=1, source_target_pairs={{0,32},{4,36},{8,40},{12,44},{16,48},{20,52},{24,56},{28,60},{32,0... | collective-permute-start | bytes 6291464 | tf_op jit(solution)/shard_map/ppermute | solution.py:10
  389.3 14.9 %collective-permute-start.9 = (f32[32,4096]{1,0:T(8,128)}, f32[32,4096]{1,0:T(8,128)S(1)}, u32[]{:S(2)}, u32[]{:S(2)}) collective-permute-start(f32[32,4096]{1,0:T(8,128)} %get-tuple-element.99), channel_id=1, source_target_pairs={{0,64},{4,68},{8,72},{12,76},{16,80},{20,84},{24,88},{28,92},{32,9... | collective-permute-start | bytes 1572872 | tf_op jit(solution)/shard_map/ppermute | solution.py:10
  441.4 9.1 collective-permute-start.12
  457.5 30.4 %collective-permute-start.14 = (f32[256,512]{0,1:T(8,128)S(1)}, f32[256,512]{0,1:T(8,128)S(1)}, u32[]{:S(2)}, u32[]{:S(2)}) collective-permute-start(f32[256,512]{0,1:T(8,128)S(1)} %maximum_select_fusion.17), channel_id=1, source_target_pairs={{0,64},{4,68},{8,72},{12,76},{16,80},{20,84},{24,88},{28,92},{32,9... | collective-permute-start | bytes 1572872 | tf_op jit(solution)/shard_map/ppermute | solution.py:10
  460.1 23.2 %all-to-all-start.2 = ((bf16[64,4,2,16]{3,2,1,0:T(2,128)(2,1)}), bf16[64,4,2,16]{3,2,1,0:T(2,128)(2,1)S(1)}, u32[]{:S(2)}, u32[]{:S(2)}) async-start(bf16[64,4,2,16]{3,2,1,0:T(2,128)(2,1)} %bitcast.45), calls=%async_computation.2 | async-start | bytes 262144 | tf_op jit(solution)/shard_map/all_to_all | solution.py:38
  484.2 142.2 %all-to-all-start.3 = ((bf16[4,2,1024]{2,1,0:T(2,128)(2,1)}), bf16[4,2,1024]{2,1,0:T(2,128)(2,1)S(1)}, u32[]{:S(2)}, u32[]{:S(2)}) async-start(bf16[4,2,1024]{2,1,0:T(2,128)(2,1)} %reshape.848), calls=%async_computation.3 | async-start | bytes 32768 | tf_op jit(solution)/shard_map/all_to_all | solution.py:37
  626.4 216.5 %all-to-all-start.4 = ((bf16[64,4,2,4608]{3,2,1,0:T(2,128)(2,1)}), bf16[64,4,2,4608]{3,2,1,0:T(2,128)(2,1)}, u32[]{:S(2)}, u32[]{:S(2)}) async-start(bf16[64,4,2,4608]{3,2,1,0:T(2,128)(2,1)} %reshape.290), calls=%async_computation.4 | async-start | bytes 9437184 | tf_op jit(solution)/shard_map/all_to_all | solution.py:31
  702.4 9.2 collective-permute-start.16
  711.9 15.1 %collective-permute-start.17 = (bf16[512,512]{1,0:T(8,128)(2,1)S(1)}, bf16[512,512]{1,0:T(8,128)(2,1)S(1)}, u32[]{:S(2)}, u32[]{:S(2)}) collective-permute-start(bf16[512,512]{1,0:T(8,128)(2,1)S(1)} %maximum_select_fusion.18), channel_id=1, source_target_pairs={{0,16},{4,20},{8,24},{12,28},{16,0},{20,4},{24,8},{28,12},{32,48},... | collective-permute-start | bytes 1572872 | tf_op jit(solution)/shard_map/ppermute | solution.py:10
  727.4 32.7 %collective-permute-start.18 = (bf16[1024,512]{1,0:T(8,128)(2,1)S(1)}, bf16[1024,512]{1,0:T(8,128)(2,1)S(1)}, u32[]{:S(2)}, u32[]{:S(2)}) collective-permute-start(bf16[1024,512]{1,0:T(8,128)(2,1)S(1)} %maximum_select_fusion.12), channel_id=1, source_target_pairs={{0,32},{4,36},{8,40},{12,44},{16,48},{20,52},{24,56},{28,60},{32,0... | collective-permute-start | bytes 3145736 | tf_op jit(solution)/shard_map/ppermute | solution.py:10
  762.0 46.6 %collective-permute-start.19 = (bf16[2048,512]{1,0:T(8,128)(2,1)}, bf16[2048,512]{1,0:T(8,128)(2,1)}, u32[]{:S(2)}, u32[]{:S(2)}) collective-permute-start(bf16[2048,512]{1,0:T(8,128)(2,1)} %maximum_select_fusion.7), channel_id=1, source_target_pairs={{0,64},{4,68},{8,72},{12,76},{16,80},{20,84},{24,88},{28,92},{32,9... | collective-permute-start | bytes 6291464 | tf_op jit(solution)/shard_map/ppermute | solution.py:10
  813.1 16.4 %collective-permute-start.20 = (f32[16,4096]{1,0:T(8,128)S(1)}, f32[16,4096]{1,0:T(8,128)S(1)}, u32[]{:S(2)}, u32[]{:S(2)}) collective-permute-start(f32[16,4096]{1,0:T(8,128)S(1)} %get-tuple-element.101), channel_id=1, source_target_pairs={{0,128},{4,132},{8,136},{12,140},{16,144},{20,148},{24,152},{28,15... | collective-permute-start | bytes 786440 | tf_op jit(solution)/shard_map/ppermute | solution.py:10
  843.6 11.4 all-to-all-start.6
  855.0 269.9 %all-to-all-start.5 = ((bf16[64,4,2,4608]{3,0,2,1:T(8,128)(2,1)}), bf16[64,4,2,4608]{3,0,2,1:T(8,128)(2,1)}, u32[]{:S(2)}, u32[]{:S(2)}) async-start(bf16[64,4,2,4608]{3,0,2,1:T(8,128)(2,1)} %copy.78), calls=%async_computation.5 | async-start | bytes 9437184 | tf_op jit(solution)/shard_map/all_to_all | solution.py:30
  871.4 92.4 %collective-permute-start.24 = (f32[64,512]{1,0:T(8,128)S(1)}, f32[64,512]{1,0:T(8,128)S(1)}, u32[]{:S(2)}, u32[]{:S(2)}) collective-permute-start(f32[64,512]{1,0:T(8,128)S(1)} %maximum_select_fusion.28), channel_id=1, source_target_pairs={{0,32},{4,36},{8,40},{12,44},{16,48},{20,52},{24,56},{28,60},{32,0... | collective-permute-start | bytes 393224 | tf_op jit(solution)/shard_map/ppermute | solution.py:10
  963.9 9.3 collective-permute-start.25
  973.2 10.8 collective-permute-start.26
  1161.8 12.3 collective-permute-start.30
  1174.6 22.6 %collective-permute-start.31 = (bf16[1024,512]{1,0:T(8,128)(2,1)S(1)}, bf16[1024,512]{1,0:T(8,128)(2,1)S(1)}, u32[]{:S(2)}, u32[]{:S(2)}) collective-permute-start(bf16[1024,512]{1,0:T(8,128)(2,1)S(1)} %maximum_select_fusion.14), channel_id=1, source_target_pairs={{0,64},{4,68},{8,72},{12,76},{16,80},{20,84},{24,88},{28,92},{32,9... | collective-permute-start | bytes 3145736 | tf_op jit(solution)/shard_map/ppermute | solution.py:10
  1197.9 45.7 %collective-permute-start.32 = (bf16[2048,512]{1,0:T(8,128)(2,1)S(1)}, bf16[2048,512]{1,0:T(8,128)(2,1)S(1)}, u32[]{:S(2)}, u32[]{:S(2)}) collective-permute-start(bf16[2048,512]{1,0:T(8,128)(2,1)S(1)} %maximum_select_fusion.8), channel_id=1, source_target_pairs={{0,128},{4,132},{8,136},{12,140},{16,144},{20,148},{24,152},{28,15... | collective-permute-start | bytes 6291464 | tf_op jit(solution)/shard_map/ppermute | solution.py:10
  (27 other events, 551.9 us)
